TPU v7x, 256 devices: a whole 4x4x8 slice. The times are simulated.
256 devices in a mesh: cfg: 2 (over y_lo), blk: 32 (over y_hi, z, core), uly: 4 (over x).
Axes of the slice: x: 4, y: 4 (y_hi: 2, y_lo: 2; y = y_hi * 2 + y_lo), z: 8, core: 2. Of those that a mesh axis runs over, the one named last changes fastest.
Arguments:
- query: bfloat16 [2, 8192, 2048], P('cfg', ('blk', 'uly')), may hold values from -6 to 6
- key: bfloat16 [2, 8192, 2048], P('cfg', ('blk', 'uly')), may hold values from -6 to 6
- value: bfloat16 [2, 8192, 2048], P('cfg', ('blk', 'uly')), may hold values from -6 to 6
- text_key: bfloat16 [2, 333, 2048], P('cfg'), may hold values from -6 to 6
- text_value: bfloat16 [2, 333, 2048], P('cfg'), may hold values from -6 to 6
- stream: bfloat16 [2, 8192, 2432], P('cfg', ('blk', 'uly')), may hold values from -30 to 30
- modulation: float32 [2, 5, 2432], P('cfg'), may hold values from -3 to 3
- out_weight: bfloat16 [2048, 2432], P(('uly', 'blk')), may hold values from -0.125 to 0.125
- final_weight: bfloat16 [2432, 64], replicated, may hold values from -0.125 to 0.125
- final_bias: float32 [64], replicated, may hold values from -3 to 3
- latents: float32 [8192, 64], P(('blk', 'uly')), may hold values from -5 to 5
- sigmas: float32 [29], replicated, may hold values from 0 to 1, as said below
- step_index: int32 [1], replicated, may hold values from 0 to 27
- patch_weight: bfloat16 [64, 2432], replicated, may hold values from -0.75 to 0.75
- position: bfloat16 [8192, 2432], P('blk'), may hold values from -1 to 1
- qkv_weight: bfloat16 [3, 2432, 2048], P(None, 'blk', 'uly'), may hold values from -0.125 to 0.125
- norm_gains: float32 [2, 64], replicated, may hold values from 0.25 to 1.75
Outputs:
- velocity: float32 [8192, 64], P(('blk', 'uly'))
- latents_next: float32 [8192, 64], P(('blk', 'uly'))
- next_qkv: bfloat16 [2, 3, 8192, 2048], P('cfg', None, 'blk', 'uly')
Inputs may be any that keep to these rules, and one draw needn't show every extreme that they name: Decreasing, with sigmas[0] = 1 and sigmas[28] = 0.
All inputs are finite; a program needn't handle non-finite values.
Results may differ from a plain program's by a relative error of at most 0.013.
Values may be sent and summed in bfloat16 or wider, within the bound.
No kernel may reach another device: no remote copies, remote signals or barrier semaphores. Data moves between devices by JAX's collectives and lax.ppermute only.
A program may use at most 128 MiB of HBM per device.

v0:
```python
import jax
import jax.numpy as jnp
from jax import lax
from jax.sharding import PartitionSpec as P

HD = 64


norm_epsilon = 1e-06
guidance_scale = 3.5


def swapped(block, axis, bit):
    count = lax.axis_size(axis)
    route = []
    for low in range(count):
        high = low | 1 << bit
        if high != low and high < count:
            route += [(low, high), (high, low)]
    return lax.ppermute(block, axis, route)


def layer_norm(matrix):
    mean = jnp.mean(matrix, axis=-1, keepdims=True)
    centred = matrix - mean
    variance = jnp.mean(centred * centred, axis=-1, keepdims=True)
    return centred * lax.rsqrt(variance + norm_epsilon)


def head_rms(matrix, gain):
    height = matrix.shape[0]
    shaped = matrix.reshape(height, -1, HD)
    squares = jnp.mean(shaped * shaped, axis=-1, keepdims=True)
    return (shaped * lax.rsqrt(squares + norm_epsilon) * gain).reshape(height, -1)


def fold_block(state, queries, block_keys, block_values):
    peak, total, summed = state
    length = block_keys.shape[0]
    shaped_keys = block_keys.reshape(length, -1, HD)
    shaped_values = block_values.reshape(length, -1, HD)
    scores = jnp.einsum(
        "hqd,khd->hqk", queries, shaped_keys, preferred_element_type=jnp.float32
    ) * HD ** (-0.5)
    new_peak = jnp.maximum(peak, jnp.max(scores, axis=-1))
    expo = jnp.exp(scores - new_peak[:, :, None])
    decay = jnp.exp(peak - new_peak)
    total = total * decay + jnp.sum(expo, axis=-1)
    summed = summed * decay[:, :, None] + jnp.einsum(
        "hqk,khd->hqd", expo.astype(jnp.bfloat16), shaped_values, preferred_element_type=jnp.float32
    )
    return (new_peak, total, summed)


def fold_keys(state, queries, block_keys, block_values):
    length = block_keys.shape[0]
    if length >= 2048 and length % 1024 == 0:

        def advance(running, both):
            return (fold_block(running, queries, both[0], both[1]), None)

        stacked_keys = block_keys.reshape(length // 1024, 1024, -1)
        stacked_values = block_values.reshape(length // 1024, 1024, -1)
        state, unused = lax.scan(advance, state, (stacked_keys, stacked_values))
        return state
    return fold_block(state, queries, block_keys, block_values)


def start_heads(query_rows, text_key, text_value, column_start):
    group_rows = query_rows.shape[0]
    width = query_rows.shape[1]
    queries = query_rows.reshape(group_rows, -1, HD).transpose(1, 0, 2)
    heads_here = queries.shape[0]
    own_text_keys = lax.dynamic_slice_in_dim(text_key, column_start, width, 1)
    own_text_values = lax.dynamic_slice_in_dim(text_value, column_start, width, 1)
    empty_state = (
        jnp.full((heads_here, group_rows), -jnp.inf, jnp.float32),
        jnp.zeros((heads_here, group_rows), jnp.float32),
        jnp.zeros((heads_here, group_rows, HD), jnp.float32),
    )
    return (queries, fold_keys(empty_state, queries, own_text_keys, own_text_values))


def finish_heads(state):
    peak, total, summed = state
    group_rows = summed.shape[1]
    return (
        (summed / total[:, :, None]).astype(jnp.bfloat16).transpose(1, 0, 2).reshape(group_rows, -1)
    )


def local(
    query,
    key,
    value,
    text_key,
    text_value,
    stream,
    modulation,
    out_weight,
    final_weight,
    final_bias,
    latents,
    sigmas,
    step_index,
    patch_weight,
    position,
    qkv_weight,
    norm_gains,
):
    query_rows, key_rows, value_rows = (
        lax.all_to_all(query[0], "uly", split_axis=1, concat_axis=0, tiled=True),
        lax.all_to_all(key[0], "uly", split_axis=1, concat_axis=0, tiled=True),
        lax.all_to_all(value[0], "uly", split_axis=1, concat_axis=0, tiled=True),
    )
    width = query_rows.shape[1]
    queries, text_state = start_heads(
        query_rows, text_key[0], text_value[0], lax.axis_index("uly") * width
    )
    attended = finish_heads(
        fold_keys(
            text_state,
            queries,
            lax.all_gather(key_rows, "blk", axis=0, tiled=True),
            lax.all_gather(value_rows, "blk", axis=0, tiled=True),
        )
    )
    out_full = lax.all_gather(out_weight, "blk", axis=0, tiled=True)
    local_rows = latents.shape[0]
    projected = lax.psum_scatter(
        jnp.dot(attended, out_full, preferred_element_type=jnp.float32).astype(jnp.bfloat16),
        "uly",
        scatter_dimension=0,
        tiled=True,
    ).astype(jnp.float32)
    params = modulation[0]
    residual = stream[0].astype(jnp.float32) + params[0] * projected
    normed = (layer_norm(residual) * (1.0 + params[2]) + params[1]).astype(jnp.bfloat16)
    predicted = jnp.dot(normed, final_weight, preferred_element_type=jnp.float32) + final_bias
    partner = swapped(predicted, "cfg", 0)
    is_first = lax.axis_index("cfg") == 0
    with_text = jnp.where(is_first, predicted, partner)
    without_text = jnp.where(is_first, partner, predicted)
    velocity = without_text + guidance_scale * (with_text - without_text)
    moment = step_index[0]
    latents_next = latents + (sigmas[moment + 1] - sigmas[moment]) * velocity
    latents_low = latents_next.astype(jnp.bfloat16)
    offset = lax.axis_index("uly") * local_rows
    own_position = lax.dynamic_slice_in_dim(position, offset, local_rows, 0)
    embedded = jnp.dot(
        latents_low, patch_weight, preferred_element_type=jnp.float32
    ) + own_position.astype(jnp.float32)
    modulated = (layer_norm(embedded) * (1.0 + params[4]) + params[3]).astype(jnp.bfloat16)
    inputs = lax.all_gather(modulated, "uly", axis=0, tiled=True)
    next_projected = jnp.einsum(
        "rd,tdc->trc",
        inputs,
        lax.all_gather(qkv_weight, "blk", axis=1, tiled=True),
        preferred_element_type=jnp.float32,
    )
    next_query = head_rms(next_projected[0], norm_gains[0])
    next_key = head_rms(next_projected[1], norm_gains[1])
    next_qkv = jnp.stack([next_query, next_key, next_projected[2]]).astype(jnp.bfloat16)[None]
    return (velocity, latents_next, next_qkv)


def solution(mesh):
    placed = (
        P("cfg", ("blk", "uly"), None),
        P("cfg", ("blk", "uly"), None),
        P("cfg", ("blk", "uly"), None),
        P("cfg", None, None),
        P("cfg", None, None),
        P("cfg", ("blk", "uly"), None),
        P("cfg", None, None),
        P(("uly", "blk"), None),
        P(),
        P(),
        P(("blk", "uly"), None),
        P(),
        P(),
        P(),
        P("blk", None),
        P(None, "blk", "uly"),
        P(),
    )
    return jax.shard_map(
        local,
        mesh=mesh,
        in_specs=placed,
        out_specs=(P(("blk", "uly"), None), P(("blk", "uly"), None), P("cfg", None, "blk", "uly")),
        check_vma=False,
    )
```

profile of v0, /device:TPU:8, one launch (start us, length us, event | category | flops | bytes accessed | tf_op | source)
XLA Modules:
  0.0 523.7 jit_solution(5137939465469573912)
XLA Ops:
  8.5 10.9 %all_to_all.54 = bf16[64,4,512]{2,0,1:T(8,128)(2,1)} all-to-all(bf16[64,4,512]{2,0,1:T(8,128)(2,1)S(1)} %copy.53), channel_id=1, replica_groups=mesh['cfg'=2,'blk'=32,'uly'=4] {'uly'}, dimensions={1} | all-to-all | bytes 524288 | tf_op jit(solution)/shard_map/all_to_all | solution.py:113
  20.6 9.7 %all_to_all.55 = bf16[64,4,512]{2,0,1:T(8,128)(2,1)} all-to-all(bf16[64,4,512]{2,0,1:T(8,128)(2,1)S(1)} %copy.54), channel_id=1, replica_groups=mesh['cfg'=2,'blk'=32,'uly'=4] {'uly'}, dimensions={1} | all-to-all | bytes 524288 | tf_op jit(solution)/shard_map/all_to_all | solution.py:114
  31.3 3.4 all-to-all-start
  37.1 4.3 all-to-all-done
  44.5 76.6 %all-gather.6.cloned.1.call-done = bf16[8192,512]{1,0:T(8,128)(2,1)} async-done(((bf16[256,512]{1,0:T(8,128)(2,1)}), bf16[8192,512]{1,0:T(8,128)(2,1)}) %all-gather.6.cloned.1.call-update) | async-done | bytes 8388624 | tf_op jit(solution)/shard_map/all_gather | solution.py:124
  121.1 100.7 %all-gather.8.cloned.1.call-done = bf16[8192,512]{1,0:T(8,128)(2,1)} async-done(((bf16[256,512]{1,0:T(8,128)(2,1)}), bf16[8192,512]{1,0:T(8,128)(2,1)}) %all-gather.8.cloned.1.call-update) | async-done | bytes 8388624 | tf_op jit(solution)/shard_map/all_gather | solution.py:125
  221.9 118.9 %while.14 = (s32[]{:T(128)}, f32[8,256]{1,0:T(8,128)S(1)}, f32[8,256]{1,0:T(8,128)S(1)}, f32[8,256,64]{1,2,0:T(8,128)}, bf16[8,1024,512]{2,1,0:T(8,128)(2,1)}, /...) while((s32[]{:T(128)}, f32[8,256]{1,0:T(8,128)S(1)}, f32[8,256]{1,0:T(8,128)S(1)}, ...), condition=%wide.region_5.6_spmd, body=%wide.region_2.5_spmd.sunk | while | flops 553914368 | bytes 76939488 | solution.py:64
  230.9 5.1 fusion.64
  239.7 2.3 bitcast_reduce_fusion.3
  245.7 5.1 fusion.64
  254.5 2.3 bitcast_reduce_fusion.3
  260.6 5.0 fusion.64
  275.4 5.1 fusion.64
  290.3 5.1 fusion.64
  299.1 2.3 bitcast_reduce_fusion.3
  305.2 5.0 fusion.64
  314.0 2.3 bitcast_reduce_fusion.3
  320.0 5.0 fusion.64
  334.9 5.0 fusion.64
  341.9 3.7 convolution_convert_fusion
  346.8 23.2 %reduce-scatter.2.cloned.1.call-done = bf16[64,2432]{1,0:T(8,128)(2,1)} async-done(((bf16[256,2432]{1,0:T(8,128)(2,1)}), bf16[64,2432]{1,0:T(8,128)(2,1)}) %reduce-scatter.2.cloned.1.call-update) | async-done | bytes 311312 | tf_op jit(solution)/shard_map/reduce_scatter | solution.py:130
  381.3 98.4 %all-gather.14.cloned.1.call-done = bf16[3,2432,512]{2,0,1:T(4,128)(2,1)} async-done(((bf16[3,76,512]{2,0,1:T(4,128)(2,1)}), bf16[3,2432,512]{2,0,1:T(4,128)(2,1)}) %all-gather.14.cloned.1.call-update) | async-done | bytes 7471120 | tf_op jit(solution)/shard_map/all_gather | solution.py:158
  479.7 26.7 %all-gather.12.cloned.1.call-done = bf16[256,2432]{1,0:T(8,128)(2,1)} async-done(((bf16[64,2432]{1,0:T(8,128)(2,1)}), bf16[256,2432]{1,0:T(8,128)(2,1)}) %all-gather.12.cloned.1.call-update) | async-done | bytes 1245200 | tf_op jit(solution)/shard_map/all_gather | solution.py:154
  506.4 6.6 %fusion.16 = f32[3,256,512]{2,1,0:T(8,128)S(1)} fusion(bf16[3,2432,512]{2,0,1:T(4,128)(2,1)} %all-gather.14.cloned.1.call-done, bf16[256,2432]{1,0:T(8,128)(2,1)} %all-gather.12.cloned.1.call-done), kind=kOutput, calls=%fused_computation.23 | convolution fusion | flops 1912602624 | bytes 10289152 | tf_op jit(solution)/shard_map/rd,tdc->trc/dot_general | solution.py:155
  (228 shorter events, 92.7 us)
Async XLA Ops:
  7.2 371.4 %copy-start = (bf16[64,2432]{1,0:T(8,128)(2,1)S(1)}, bf16[64,2432]{1,0:T(8,128)(2,1)}, u32[]{:S(2)}) copy-start(bf16[64,2432]{1,0:T(8,128)(2,1)} %param.32) | copy-start | bytes 933892
  7.2 23.2 %copy-start.8 = (bf16[1,64,2048]{2,1,0:T(8,128)(2,1)S(1)}, bf16[1,64,2048]{2,1,0:T(8,128)(2,1)}, u32[]{:S(2)}) copy-start(bf16[1,64,2048]{2,1,0:T(8,128)(2,1)} %param.19) | copy-start | bytes 786436
  7.2 113.9 %all-gather.6.cloned.1.call-start = ((), (), s32[]{:S(2)}) async-start(), calls=%async_computation.4 | async-start | bytes 8650752 | tf_op jit(solution)/shard_map/all_gather | solution.py:124
  19.4 202.5 %all-gather.8.cloned.1.call-start = ((), (), s32[]{:S(2)}) async-start(), calls=%async_computation.5 | async-start | bytes 8650752 | tf_op jit(solution)/shard_map/all_gather | solution.py:125
  31.3 10.1 %all-to-all-start = ((bf16[64,4,512]{2,0,1:T(8,128)(2,1)}), bf16[64,4,512]{2,0,1:T(8,128)(2,1)S(1)}, u32[]{:S(2)}, u32[]{:S(2)}) async-start(bf16[64,4,512]{2,0,1:T(8,128)(2,1)} %copy.50), calls=%async_computation | async-start | bytes 524288 | tf_op jit(solution)/shard_map/all_to_all | solution.py:112
  34.8 307.1 %all-gather.10.cloned.1.call-start = ((), (), s32[]{:S(2)}) async-start(), calls=%async_computation.6 | async-start | bytes 2568192 | tf_op jit(solution)/shard_map/all_gather | solution.py:128
  35.5 334.5 %reduce-scatter.2.cloned.1.call-start = ((), (), s32[]{:S(2)}) async-start(), calls=%async_computation.7 | async-start | bytes 1556480 | tf_op jit(solution)/shard_map/reduce_scatter | solution.py:130
  230.8 5.9 %copy-start.5 = (bf16[8,256,64]{1,2,0:T(8,128)(2,1)S(1)}, bf16[8,256,64]{1,2,0:T(8,128)(2,1)}, u32[]{:S(2)}) copy-start(bf16[8,256,64]{1,2,0:T(8,128)(2,1)} %copy-done.4) | copy-start | bytes 786436 | tf_op jit(solution)/shard_map/while
  245.7 5.9 %copy-start.5 = (bf16[8,256,64]{1,2,0:T(8,128)(2,1)S(1)}, bf16[8,256,64]{1,2,0:T(8,128)(2,1)}, u32[]{:S(2)}) copy-start(bf16[8,256,64]{1,2,0:T(8,128)(2,1)} %copy-done.4) | copy-start | bytes 786436 | tf_op jit(solution)/shard_map/while
  260.6 5.9 %copy-start.5 = (bf16[8,256,64]{1,2,0:T(8,128)(2,1)S(1)}, bf16[8,256,64]{1,2,0:T(8,128)(2,1)}, u32[]{:S(2)}) copy-start(bf16[8,256,64]{1,2,0:T(8,128)(2,1)} %copy-done.4) | copy-start | bytes 786436 | tf_op jit(solution)/shard_map/while
  275.4 5.9 %copy-start.5 = (bf16[8,256,64]{1,2,0:T(8,128)(2,1)S(1)}, bf16[8,256,64]{1,2,0:T(8,128)(2,1)}, u32[]{:S(2)}) copy-start(bf16[8,256,64]{1,2,0:T(8,128)(2,1)} %copy-done.4) | copy-start | bytes 786436 | tf_op jit(solution)/shard_map/while
  290.3 5.9 %copy-start.5 = (bf16[8,256,64]{1,2,0:T(8,128)(2,1)S(1)}, bf16[8,256,64]{1,2,0:T(8,128)(2,1)}, u32[]{:S(2)}) copy-start(bf16[8,256,64]{1,2,0:T(8,128)(2,1)} %copy-done.4) | copy-start | bytes 786436 | tf_op jit(solution)/shard_map/while
  320.0 5.9 %copy-start.5 = (bf16[8,256,64]{1,2,0:T(8,128)(2,1)S(1)}, bf16[8,256,64]{1,2,0:T(8,128)(2,1)}, u32[]{:S(2)}) copy-start(bf16[8,256,64]{1,2,0:T(8,128)(2,1)} %copy-done.4) | copy-start | bytes 786436 | tf_op jit(solution)/shard_map/while
  334.9 5.9 %copy-start.5 = (bf16[8,256,64]{1,2,0:T(8,128)(2,1)S(1)}, bf16[8,256,64]{1,2,0:T(8,128)(2,1)}, u32[]{:S(2)}) copy-start(bf16[8,256,64]{1,2,0:T(8,128)(2,1)} %copy-done.4) | copy-start | bytes 786436 | tf_op jit(solution)/shard_map/while
  341.9 28.1 %copy-start.6 = (bf16[1,64,2432]{2,1,0:T(8,128)(2,1)S(1)}, bf16[1,64,2432]{2,1,0:T(8,128)(2,1)}, u32[]{:S(2)}) copy-start(bf16[1,64,2432]{2,1,0:T(8,128)(2,1)} %param.24) | copy-start | bytes 933892
  345.6 26.8 %copy-start.15 = (bf16[2432,64]{0,1:T(8,128)(2,1)S(1)}, bf16[2432,64]{0,1:T(8,128)(2,1)}, u32[]{:S(2)}) copy-start(bf16[2432,64]{0,1:T(8,128)(2,1)} %param.27) | copy-start | bytes 933892
  345.6 26.9 %copy-start.16 = (f32[64]{0:T(128)S(1)}, f32[64]{0:T(128)}, u32[]{:S(2)}) copy-start(f32[64]{0:T(128)} %param.28) | copy-start | bytes 772
  345.6 29.6 %copy-start.13 = (f32[29]{0:T(128)S(1)}, f32[29]{0:T(128)}, u32[]{:S(2)}) copy-start(f32[29]{0:T(128)} %param.30) | copy-start | bytes 352
  345.6 32.3 %copy-start.12 = (f32[64,64]{1,0:T(8,128)S(1)}, f32[64,64]{1,0:T(8,128)}, u32[]{:S(2)}) copy-start(f32[64,64]{1,0:T(8,128)} %param.29) | copy-start | bytes 49156
  345.6 134.1 %all-gather.14.cloned.1.call-start = ((), (), s32[]{:S(2)}) async-start(), calls=%async_computation.9 | async-start | bytes 10272768 | tf_op jit(solution)/shard_map/all_gather | solution.py:158
  346.6 159.8 %all-gather.12.cloned.1.call-start = ((), (), s32[]{:S(2)}) async-start(), calls=%async_computation.8 | async-start | bytes 1556480 | tf_op jit(solution)/shard_map/all_gather | solution.py:154
  371.2 9.9 %copy-start.14 = (f32[2,64]{1,0:T(2,128)S(1)}, f32[2,64]{1,0:T(2,128)}, u32[]{:S(2)}) copy-start(f32[2,64]{1,0:T(2,128)} %param.35) | copy-start | bytes 1540
  373.8 4.2 collective-permute-start
  378.6 134.5 %copy-start.10 = (f32[64,64]{1,0:T(8,128)}, f32[64,64]{1,0:T(8,128)S(1)}, u32[]{:S(2)}) copy-start(f32[64,64]{1,0:T(8,128)S(1)} %get-tuple-element.85) | copy-start | bytes 49156
  (36 other events, 83.2 us)
Sparse Core Ops, SparseCore 0:
  19.5 101.5 all-gather.5
  123.9 97.9 all-gather.7
  224.6 77.7 all-gather.9
  345.7 24.2 reduce-scatter.1
  373.6 106.0 all-gather.13
  481.5 24.8 all-gather.11
where the time goes:
time: 525 us; the launch traced here: 524 us
  waiting for transfers between devices  332 us (63%)
  matrix products  73.5 us (14%)
  local copies, waits for them, and re-layouts  57.8 us (11%)
  blocking collectives  20.6 us (4%)
  other arithmetic  18.6 us (4%)
  between operations  16.5 us (3%)
    all_gather x1, waiting for transfers between devices, local(): lax.all_gather(value_rows, 'blk', axis=0, tiled=True)  101 us
    all_gather x1, waiting for transfers between devices, local(): lax.all_gather(qkv_weight, 'blk', axis=1, tiled=True)  98.4 us
    all_gather x1, waiting for transfers between devices, local(): lax.all_gather(key_rows, 'blk', axis=0, tiled=True)  76.6 us
    dot_general x9, matrix products, fold_block(): jnp.einsum('hqk,khd->hqd', expo.astype(jnp.bfloat16), shaped_values, pref...  41.8 us
    all_gather x1, waiting for transfers between devices, local(): inputs = lax.all_gather(modulated, 'uly', axis=0, tiled=True)  26.7 us
    while x88, local copies, waits for them, and re-layouts  26.2 us
    reduce_scatter x1, waiting for transfers between devices, local(): lax.psum_scatter(jnp.dot(attended, out_full, preferred_element_type=jnp.f...  23.2 us
    dynamic_slice x24, local copies, waits for them, and re-layouts, fold_keys(): state, unused = lax.scan(advance, state, (stacked_keys, stacked_values))  22 us
  transfers between devices with their start and end apart: 8, of which 7 were waited for; matrix products, arithmetic and copies ran while one was open for 20% of the time, Pallas kernels for 0%

commit v1 on v0

v1 whole, which is shorter than its diff:
```python
import functools

import jax
import jax.numpy as jnp
from jax import lax
from jax.experimental import pallas as pl
from jax.experimental.pallas import tpu as pltpu
from jax.sharding import Mesh, PartitionSpec as P

HD = 64
norm_epsilon = 1e-06
guidance_scale = 3.5
bf16 = jnp.bfloat16
f32 = jnp.float32
KEY_BLOCK = 1024


def params(limit_mib=56, **more):
    return pltpu.CompilerParams(vmem_limit_bytes=limit_mib * 2**20, **more)


def whole(shape):
    return pl.BlockSpec(shape, lambda *_: (0,) * len(shape))


def half_swap(block):
    return pltpu.roll(block.astype(f32), 64, 1).astype(block.dtype)


def low_lanes(shape):
    return lax.broadcasted_iota(jnp.int32, shape, len(shape) - 1) < 64


def pack_kernel(zs, us, head_ref, query_ref, key_ref, value_ref, text_key_ref, text_value_ref, send_ref, text_ref):
    rows = query_ref.shape[1]
    half = rows // 2
    low = low_lanes((rows, 128))
    low_half = low_lanes((half, 128))
    for pair in range(zs * us // 2):
        lanes = slice(128 * pair, 128 * pair + 128)
        keys = key_ref[0, :, lanes]
        values = value_ref[0, :, lanes]
        queries = query_ref[0, :, lanes] * 0.125
        first, second = queries[:half], queries[half:]
        for odd in range(2):
            head = 2 * pair + odd
            place = (head % zs) * us + head // zs
            if odd:
                both = jnp.where(low, half_swap(keys), values)
                folded = jnp.where(low_half, half_swap(first), second)
            else:
                both = jnp.where(low, keys, half_swap(values))
                folded = jnp.where(low_half, first, half_swap(second))
            send_ref[place, :rows, :] = both
            send_ref[place, rows:, :] = folded
    odd_head = lax.rem(head_ref[0], 2) == 1
    text_rows = text_key_ref.shape[1]
    text_low = low_lanes((text_rows, 128))
    keys = text_key_ref[0]
    values = text_value_ref[0]
    both = jnp.where(
        text_low,
        jnp.where(odd_head, half_swap(keys), keys),
        jnp.where(odd_head, values, half_swap(values)),
    )
    text_ref[...] = jnp.zeros(text_ref.shape, bf16)
    text_ref[:text_rows, :] = both


def pack(zs, us, head, query, key, value, text_key, text_value):
    rows = query.shape[1]
    text_rows = text_key.shape[1]
    text_padded = -(-text_rows // 128) * 128
    text_spec = pl.BlockSpec((1, text_rows, 128), lambda i, head: (0, 0, head[0] // 2))
    return pl.pallas_call(
        functools.partial(pack_kernel, zs, us),
        grid_spec=pltpu.PrefetchScalarGridSpec(
            num_scalar_prefetch=1,
            grid=(1,),
            in_specs=[whole(query.shape), whole(key.shape), whole(value.shape), text_spec, text_spec],
            out_specs=[whole((zs * us, rows + rows // 2, 128)), whole((text_padded, 128))],
        ),
        out_shape=[
            jax.ShapeDtypeStruct((zs * us, rows + rows // 2, 128), bf16),
            jax.ShapeDtypeStruct((text_padded, 128), bf16),
        ],
        compiler_params=params(),
        name="pack",
    )(head, query, key, value, text_key, text_value)


def value_rows(both):
    return jnp.concatenate([jnp.transpose(both)[64:], jnp.ones((16, both.shape[0]), bf16)], axis=0)


def scores_of(both, queries):
    return lax.dot_general(both, queries, (((1,), (1,)), ((), ())), preferred_element_type=f32)


def fold(peak, mixed, both, queries):
    scores = scores_of(both, queries)
    new_peak = jnp.maximum(peak, jnp.max(scores, axis=0, keepdims=True))
    weights = jnp.exp(scores - new_peak).astype(bf16)
    mixed = mixed * jnp.exp(peak - new_peak) + jnp.dot(value_rows(both), weights, preferred_element_type=f32)
    return new_peak, mixed


def first_kernel(text_count, pieces_ref, text_ref, both_ref, queries_ref, peak_ref, mixed_ref):
    step = pl.program_id(0)

    @pl.when(step == 0)
    def _():
        count, height, _ = pieces_ref.shape
        half = height // 3
        folded = pieces_ref[:, 2 * half :, :].reshape(count * half, 128)
        low = low_lanes(folded.shape)
        zero = jnp.zeros_like(folded)
        first = jnp.where(low, folded, zero).reshape(count, half, 128)
        second = jnp.where(low, half_swap(folded), zero).reshape(count, half, 128)
        queries = jnp.concatenate([first, second], axis=1).reshape(count * 2 * half, 128)
        queries_ref[...] = queries
        text = text_ref[...]
        scores = scores_of(text, queries)
        kept = lax.broadcasted_iota(jnp.int32, scores.shape, 0) < text_count
        scores = jnp.where(kept, scores, -1e30)
        peak = jnp.max(scores, axis=0, keepdims=True)
        weights = jnp.exp(scores - peak).astype(bf16)
        peak_ref[...] = peak
        mixed_ref[...] = jnp.dot(value_rows(text), weights, preferred_element_type=f32)

    peak_ref[...], mixed_ref[...] = fold(peak_ref[...], mixed_ref[...], both_ref[...], queries_ref[...])


def first_attend(text_count, pieces, text, both):
    count, height, _ = pieces.shape
    total = count * (height // 3) * 2
    return pl.pallas_call(
        functools.partial(first_kernel, text_count),
        grid=(both.shape[0] // KEY_BLOCK,),
        in_specs=[whole(pieces.shape), whole(text.shape), pl.BlockSpec((KEY_BLOCK, 128), lambda i: (i, 0))],
        out_specs=[whole((total, 128)), whole((1, total)), whole((80, total))],
        out_shape=[
            jax.ShapeDtypeStruct((total, 128), bf16),
            jax.ShapeDtypeStruct((1, total), f32),
            jax.ShapeDtypeStruct((80, total), f32),
        ],
        compiler_params=params(),
        name="attend_first",
    )(pieces, text, both)


def next_kernel(queries_ref, peak_in_ref, mixed_in_ref, both_ref, peak_ref, mixed_ref):
    @pl.when(pl.program_id(0) == 0)
    def _():
        peak_ref[...] = peak_in_ref[...]
        mixed_ref[...] = mixed_in_ref[...]

    peak_ref[...], mixed_ref[...] = fold(peak_ref[...], mixed_ref[...], both_ref[...], queries_ref[...])


def next_attend(queries, peak, mixed, both):
    return pl.pallas_call(
        next_kernel,
        grid=(both.shape[0] // KEY_BLOCK,),
        in_specs=[
            whole(queries.shape),
            whole(peak.shape),
            whole(mixed.shape),
            pl.BlockSpec((KEY_BLOCK, 128), lambda i: (i, 0)),
        ],
        out_specs=[whole(peak.shape), whole(mixed.shape)],
        out_shape=[jax.ShapeDtypeStruct(peak.shape, f32), jax.ShapeDtypeStruct(mixed.shape, f32)],
        compiler_params=params(),
        name="attend_next",
    )(queries, peak, mixed, both)


def last_kernel(steps, queries_ref, peak_in_ref, mixed_in_ref, one_ref, two_ref, out_ref, peak_ref, mixed_ref):
    step = pl.program_id(0)

    @pl.when(step == 0)
    def _():
        peak_ref[...] = peak_in_ref[...]
        mixed_ref[...] = mixed_in_ref[...]

    both = jnp.where(step < steps, one_ref[...], two_ref[...])
    peak_ref[...], mixed_ref[...] = fold(peak_ref[...], mixed_ref[...], both, queries_ref[...])

    @pl.when(step == 2 * steps - 1)
    def _():
        mixed = mixed_ref[...]
        attended = (mixed[:64] / mixed[64:65]).astype(bf16)
        width = out_ref.shape[2]
        for place in range(out_ref.shape[0]):
            out_ref[place] = attended[:, place * width : place * width + width]


def last_attend(zs, queries, peak, mixed, one, two):
    steps = one.shape[0] // KEY_BLOCK
    total = queries.shape[0]
    return pl.pallas_call(
        functools.partial(last_kernel, steps),
        grid=(2 * steps,),
        in_specs=[
            whole(queries.shape),
            whole(peak.shape),
            whole(mixed.shape),
            pl.BlockSpec((KEY_BLOCK, 128), lambda i: (jnp.minimum(i, steps - 1), 0)),
            pl.BlockSpec((KEY_BLOCK, 128), lambda i: (jnp.maximum(i - steps, 0), 0)),
        ],
        out_specs=whole((zs, 64, total // zs)),
        out_shape=jax.ShapeDtypeStruct((zs, 64, total // zs), bf16),
        scratch_shapes=[pltpu.VMEM(peak.shape, f32), pltpu.VMEM(mixed.shape, f32)],
        compiler_params=params(),
        name="attend_last",
    )(queries, peak, mixed, one, two)


def project_kernel(place_ref, attended_ref, weight_ref, *refs):
    outs, held = refs[:-1], refs[-1]
    heads, _, tokens = attended_ref.shape
    attended = jnp.transpose(attended_ref[...].reshape(heads * 64, tokens))
    slabs, sides, rows, width = weight_ref.shape
    depth = slabs * rows
    total = jnp.zeros((tokens, width), f32)
    for side in range(sides):
        part = weight_ref[:, side].reshape(depth, width)
        total += jnp.dot(attended[:, side * depth : side * depth + depth], part, preferred_element_type=f32)
    held[...] = total.astype(bf16)
    count = len(outs)
    size = tokens // count
    for step, out_ref in enumerate(outs):
        start = pl.multiple_of(lax.rem(place_ref[0] + step, count) * size, size)
        out_ref[...] = held[pl.ds(start, size), :]


def project(us, place, attended, weight):
    tokens = attended.shape[2]
    width = weight.shape[-1]
    piece = (tokens // us, width)
    return pl.pallas_call(
        project_kernel,
        grid_spec=pltpu.PrefetchScalarGridSpec(
            num_scalar_prefetch=1,
            grid=(1,),
            in_specs=[whole(attended.shape), whole(weight.shape)],
            out_specs=[whole(piece)] * us,
            scratch_shapes=[pltpu.VMEM((tokens, width), bf16)],
        ),
        out_shape=[jax.ShapeDtypeStruct(piece, bf16)] * us,
        compiler_params=params(),
        name="project",
    )(place, attended, weight)


def layer_norm(matrix):
    mean = jnp.mean(matrix, axis=-1, keepdims=True)
    centred = matrix - mean
    variance = jnp.mean(centred * centred, axis=-1, keepdims=True)
    return centred * lax.rsqrt(variance + norm_epsilon)


def predict_kernel(stream_ref, modulation_ref, weight_ref, bias_ref, *refs):
    pieces, out_ref = refs[:-1], refs[-1]
    projected = pieces[0][...].astype(f32)
    for piece in pieces[1:]:
        projected += piece[...].astype(f32)
    gate = modulation_ref[0, 0:1, :]
    shift = modulation_ref[0, 1:2, :]
    scale = modulation_ref[0, 2:3, :]
    residual = stream_ref[0].astype(f32) + gate * projected
    normed = (layer_norm(residual) * (1.0 + scale) + shift).astype(bf16)
    out_ref[...] = jnp.dot(normed, weight_ref[...], preferred_element_type=f32) + bias_ref[...]


def predict(stream, modulation, weight, bias, pieces):
    return pl.pallas_call(
        predict_kernel,
        out_shape=jax.ShapeDtypeStruct((stream.shape[1], weight.shape[1]), f32),
        compiler_params=params(),
        name="predict",
    )(stream, modulation, weight, bias, *pieces)


def next_projection_kernel(
    place_ref, patch_ref, position_ref, modulation_ref, weight_ref, gains_ref, *refs
):
    lows, out_ref, latents, inputs = refs[:-3], refs[-3], refs[-2], refs[-1]
    kind = pl.program_id(0)

    @pl.when(kind == 0)
    def _():
        count = len(lows)
        size = lows[0].shape[0]
        for step, low_ref in enumerate(lows):
            start = pl.multiple_of(lax.rem(place_ref[0] + count - step, count) * size, size)
            latents[pl.ds(start, size), :] = low_ref[...].astype(f32)
        embedded = jnp.dot(
            latents[...].astype(bf16), patch_ref[...], preferred_element_type=f32
        ) + position_ref[...].astype(f32)
        shift = modulation_ref[0, 3:4, :]
        scale = modulation_ref[0, 4:5, :]
        inputs[...] = (layer_norm(embedded) * (1.0 + scale) + shift).astype(bf16)

    product = jnp.dot(inputs[...], weight_ref[...], preferred_element_type=f32)

    @pl.when(kind < 2)
    def _():
        gain = jnp.where(kind == 0, gains_ref[0:1, :], gains_ref[1:2, :])
        low = low_lanes((product.shape[0], 128))
        for pair in range(product.shape[1] // 128):
            lanes = slice(128 * pair, 128 * pair + 128)
            block = product[:, lanes]
            squares = block * block
            left = jnp.sum(jnp.where(low, squares, 0.0), axis=-1, keepdims=True)
            right = jnp.sum(jnp.where(low, 0.0, squares), axis=-1, keepdims=True)
            mean = jnp.where(low, left, right) * (1.0 / HD)
            out_ref[0, 0, :, lanes] = (block * lax.rsqrt(mean + norm_epsilon) * gain).astype(bf16)

    @pl.when(kind == 2)
    def _():
        out_ref[0, 0] = product.astype(bf16)


def next_projection(place, lows, patch_weight, position, modulation, weight, gains):
    tokens, depth = position.shape
    columns = weight.shape[1] // 3
    return pl.pallas_call(
        next_projection_kernel,
        grid_spec=pltpu.PrefetchScalarGridSpec(
            num_scalar_prefetch=1,
            grid=(3,),
            in_specs=[
                whole(patch_weight.shape),
                whole(position.shape),
                whole(modulation.shape),
                pl.BlockSpec((depth, columns), lambda i, place: (0, i)),
                whole(gains.shape),
            ]
            + [whole(low.shape) for low in lows],
            out_specs=pl.BlockSpec((1, 1, tokens, columns), lambda i, place: (0, i, 0, 0)),
            scratch_shapes=[
                pltpu.VMEM((tokens, lows[0].shape[1]), f32),
                pltpu.VMEM((tokens, depth), bf16),
            ],
        ),
        out_shape=jax.ShapeDtypeStruct((1, 3, tokens, columns), bf16),
        compiler_params=params(),
        name="next_projection",
    )(place, patch_weight, position, modulation, weight, gains, *lows)


def turned(block, axis, step):
    count = lax.axis_size(axis)
    return lax.ppermute(block, axis, [(i, (i + step) % count) for i in range(count)])


def both_sides(block):
    other = turned(block, "yh", 1)
    first = lax.axis_index("yh") == 0
    return jnp.stack([jnp.where(first, block, other), jnp.where(first, other, block)])


def local(
    query,
    key,
    value,
    text_key,
    text_value,
    stream,
    modulation,
    out_weight,
    final_weight,
    final_bias,
    latents,
    sigmas,
    step_index,
    patch_weight,
    position,
    qkv_weight,
    norm_gains,
):
    zs, us = lax.axis_size("z"), lax.axis_size("uly")
    z, u = lax.axis_index("z"), lax.axis_index("uly")
    place = u.astype(jnp.int32).reshape(1)
    head = (zs * u + z).astype(jnp.int32).reshape(1)

    with jax.named_scope("weights"):
        out_gathered = lax.all_gather(both_sides(out_weight), ("z", "core"), axis=0)
        kinds, slab, columns = qkv_weight.shape
        flat_weight = qkv_weight.transpose(1, 0, 2).reshape(slab, kinds * columns)
        qkv_gathered = lax.all_gather(both_sides(flat_weight), ("z", "core"), axis=0)
        qkv_full = qkv_gathered.transpose(1, 0, 2, 3).reshape(-1, kinds * columns)

    with jax.named_scope("attention"):
        send, text = pack(zs, us, head, query, key, value, text_key, text_value)
        pieces = lax.all_to_all(send, ("z", "uly"), split_axis=0, concat_axis=0, tiled=True)
        rows = query.shape[1]
        own = pieces[:, :rows, :].reshape(zs * us * rows, 128)
        across = turned(own, "yh", 1)
        beside = turned(own, "core", 1)
        queries, peak, mixed = first_attend(text_key.shape[1], pieces, text, own)
        diagonal = turned(across, "core", 1)
        peak, mixed = next_attend(queries, peak, mixed, beside)
        sent = last_attend(zs, queries, peak, mixed, across, diagonal)
        attended = lax.all_to_all(sent, "z", split_axis=0, concat_axis=0, tiled=True)

    with jax.named_scope("prediction"):
        pieces = project(us, place, attended, out_gathered)
        pieces = [pieces[0]] + [turned(pieces[step], "uly", step) for step in range(1, us)]
        predicted = predict(stream, modulation, final_weight, final_bias.reshape(1, -1), pieces)
        partner = turned(predicted, "cfg", 1)
        is_first = lax.axis_index("cfg") == 0
        with_text = jnp.where(is_first, predicted, partner)
        without_text = jnp.where(is_first, partner, predicted)
        velocity = without_text + guidance_scale * (with_text - without_text)
        moment = step_index[0]
        latents_next = latents + (sigmas[moment + 1] - sigmas[moment]) * velocity
        latents_low = latents_next.astype(bf16)

    with jax.named_scope("next"):
        lows = [latents_low] + [turned(latents_low, "uly", step) for step in range(1, us)]
        gains = jnp.concatenate([norm_gains, norm_gains], axis=1)
        next_qkv = next_projection(place, lows, patch_weight, position, modulation, qkv_full, gains)
    return (velocity, latents_next, next_qkv)


def solution(mesh):
    sizes = dict(mesh.shape)
    fine = Mesh(
        mesh.devices.reshape(sizes["cfg"], 2, sizes["blk"] // 4, 2, sizes["uly"]),
        ("cfg", "yh", "z", "core", "uly"),
    )
    blk = ("yh", "z", "core")
    tokens = blk + ("uly",)
    placed = (
        P("cfg", tokens, None),
        P("cfg", tokens, None),
        P("cfg", tokens, None),
        P("cfg", None, None),
        P("cfg", None, None),
        P("cfg", tokens, None),
        P("cfg", None, None),
        P(("uly",) + blk, None),
        P(),
        P(),
        P(tokens, None),
        P(),
        P(),
        P(),
        P(blk, None),
        P(None, blk, "uly"),
        P(),
    )
    return jax.shard_map(
        local,
        mesh=fine,
        in_specs=placed,
        out_specs=(P(tokens, None), P(tokens, None), P("cfg", None, blk, "uly")),
        check_vma=False,
    )
```

time: 525 us -> 201 us (0.38)
  waiting for transfers between devices: 332 us -> 32.9 us
  matrix products: 73.5 us -> 0 us
  Pallas kernels: 0 us -> 49.1 us
  blocking collectives: 20.6 us -> 56.6 us
  local copies, waits for them, and re-layouts: 57.8 us -> 23.2 us
  other arithmetic: 18.6 us -> 4.48 us
  starting transfers between devices: 4.46 us -> 17.9 us
    all_gather x5 -> x2, waiting for transfers between devices: 302 us -> 0.01 us  [the longest x1 0.01 us: local(): out_gathered = lax.all_gather(both_sides(out_weight), ('z', 'core'), axis=0)]
    dot_general x22 -> x0, matrix products: 73.5 us -> none  [the longest x9 41.8 us: fold_block(): jnp.einsum('hqk,khd->hqd', expo.astype(jnp.bfloat16), shaped_values, pref...]
    pallas_call x0 -> x7, Pallas kernels: none -> 49.1 us  [the longest x1 14.4 us: last_attend(): pl.pallas_call(functools.partial(last_kernel, steps), grid=(2 * steps,),...]
    all_to_all x2, blocking collectives: 20.6 us -> 56.6 us  [the longest x1 39.8 us: local(): lax.all_to_all(send, ('z', 'uly'), split_axis=0, concat_axis=0, tiled=True)]
    ppermute x1 -> x12, waiting for transfers between devices: 0.8 us -> 32.8 us  [turned(): lax.ppermute(block, axis, [(i, (i + step) % count) for i in range(count)])]
    while x88 -> x0, local copies, waits for them, and re-layouts: 26.2 us -> none
    dynamic_slice x27 -> x0, local copies, waits for them, and re-layouts: 23.6 us -> none  [the longest x24 22 us: fold_keys(): state, unused = lax.scan(advance, state, (stacked_keys, stacked_values))]
    reduce_scatter x1 -> x0, waiting for transfers between devices: 23.2 us -> none  [local(): lax.psum_scatter(jnp.dot(attended, out_full, preferred_element_type=jnp.f...]
  transfers between devices with their start and end apart: 8 -> 14, of which waited for: 7 -> 6; matrix products, arithmetic and copies ran while one was open for 20% -> 11% of each run, Pallas kernels for 0% -> 21%
where the time goes in v1:
time: 201 us; the launch traced here: 200 us
  blocking collectives  56.6 us (28%)
  Pallas kernels  49.1 us (24%)
  waiting for transfers between devices  32.9 us (16%)
  local copies, waits for them, and re-layouts  23.2 us (12%)
  starting transfers between devices  17.9 us (9%)
  between operations  16.1 us (8%)
  other arithmetic  4.48 us (2%)
    all_to_all x1, blocking collectives, local(): lax.all_to_all(send, ('z', 'uly'), split_axis=0, concat_axis=0, tiled=True)  39.8 us
    ppermute x12, waiting for transfers between devices, turned(): lax.ppermute(block, axis, [(i, (i + step) % count) for i in range(count)])  32.8 us
    ppermute x12, starting transfers between devices, turned(): lax.ppermute(block, axis, [(i, (i + step) % count) for i in range(count)])  17.8 us
    all_to_all x1, blocking collectives, local(): lax.all_to_all(sent, 'z', split_axis=0, concat_axis=0, tiled=True)  16.8 us
    pallas_call x1, Pallas kernels, last_attend(): pl.pallas_call(functools.partial(last_kernel, steps), grid=(2 * steps,),...  14.4 us
    pallas_call x1, Pallas kernels, first_attend(): pl.pallas_call(functools.partial(first_kernel, text_count), grid=(both.sh...  9.46 us
    reshape x1, local copies, waits for them, and re-layouts, local(): qkv_full = qkv_gathered.transpose(1, 0, 2, 3).reshape(-1, kinds * columns)  8.9 us
    pallas_call x1, Pallas kernels, next_attend(): pl.pallas_call(next_kernel, grid=(both.shape[0] // KEY_BLOCK,), in_specs=...  8.23 us
  transfers between devices with their start and end apart: 14, of which 6 were waited for; matrix products, arithmetic and copies ran while one was open for 11% of the time, Pallas kernels for 21%

profile of v1, /device:TPU:8, one launch (start us, length us, event | category | flops | bytes accessed | tf_op | source)
XLA Modules:
  0.0 200.2 jit_solution(6945639785687656150)
XLA Ops:
  7.2 2.4 %collective-permute-start.3 = (bf16[16,2432]{1,0:T(8,128)(2,1)}, bf16[16,2432]{1,0:T(8,128)(2,1)S(1)}, u32[]{:S(2)}, u32[]{:S(2)}) collective-permute-start(bf16[16,2432]{1,0:T(8,128)(2,1)} %param.24), channel_id=1, source_target_pairs={{0,64},{64,0},{1,65},{65,1},{2,66},{66,2},{3,67},{67,3},{4,68},{68... | collective-permute-start | bytes 233480 | tf_op jit(solution)/shard_map/weights/ppermute | solution.py:355
  9.6 3.8 %collective-permute-done.3 = bf16[16,2432]{1,0:T(8,128)(2,1)S(1)} collective-permute-done((bf16[16,2432]{1,0:T(8,128)(2,1)}, bf16[16,2432]{1,0:T(8,128)(2,1)S(1)}, u32[]{:S(2)}, u32[]{:S(2)}) %collective-permute-start.3) | collective-permute-done | bytes 77856 | tf_op jit(solution)/shard_map/weights/ppermute | solution.py:355
  16.4 2.4 %collective-permute-start.8 = (bf16[76,1536]{1,0:T(8,128)(2,1)S(1)}, bf16[76,1536]{1,0:T(8,128)(2,1)S(1)}, u32[]{:S(2)}, u32[]{:S(2)}) collective-permute-start(bf16[76,1536]{1,0:T(8,128)(2,1)S(1)} %bitcast.33), channel_id=1, source_target_pairs={{0,64},{64,0},{1,65},{65,1},{2,66},{66,2},{3,67},{67,3},{4,68},{68... | collective-permute-start | bytes 700424 | tf_op jit(solution)/shard_map/weights/ppermute | solution.py:355
  18.8 5.8 %collective-permute-done.8 = bf16[76,1536]{1,0:T(8,128)(2,1)S(1)} collective-permute-done((bf16[76,1536]{1,0:T(8,128)(2,1)S(1)}, bf16[76,1536]{1,0:T(8,128)(2,1)S(1)}, u32[]{:S(2)}, u32[]{:S(2)}) %collective-permute-start.8) | collective-permute-done | bytes 233504 | tf_op jit(solution)/shard_map/weights/ppermute | solution.py:355
  25.5 2.4 %pack.1 = (bf16[32,96,128]{2,1,0:T(8,128)(2,1)}, bf16[384,128]{1,0:T(8,128)(2,1)}) custom-call(s32[1]{0:T(128)} %bitcast.2.head_ref, bf16[1,64,2048]{2,1,0:T(8,128)(2,1)} %query_ref.1, bf16[1,64,2048]{2,1,0:T(8,128)(2,1)} %key_ref.1, bf16[1,64,2048]{2,1,0:T(8,128)(2,1)} %value_ref.1, bf16[1,333,2048]{2,1,0:T(8,128)(2,1)} %text_key_ref.1, ...), custom_call_target="tpu_custom_call" | custom-call | tf_op jit(solution)/shard_map/attention/pack/pallas_call | solution.py:75
  27.9 39.8 %all_to_all.10.pieces_ref = bf16[32,96,128]{2,1,0:T(8,128)(2,1)S(1)} all-to-all(bf16[32,96,128]{2,1,0:T(8,128)(2,1)} %get-tuple-element.14), channel_id=1, replica_groups=mesh['cfg'=2,'yh'=2,'z'=8,'core'=2,'uly'=4] {'z','uly'}, dimensions={0} | all-to-all | bytes 1572864 | tf_op jit(solution)/shard_map/attention/all_to_all | solution.py:397
  67.7 2.2 %collective-permute-start.1 = (bf16[2048,128]{1,0:T(8,128)(2,1)S(1)}, bf16[2048,128]{1,0:T(8,128)(2,1)S(1)}, u32[]{:S(2)}, u32[]{:S(2)}) collective-permute-start(bf16[2048,128]{1,0:T(8,128)(2,1)S(1)} %bitcast.29), channel_id=1, source_target_pairs={{0,64},{64,0},{1,65},{65,1},{2,66},{66,2},{3,67},{67,3},{4,68},{68... | collective-permute-start | bytes 1572872 | tf_op jit(solution)/shard_map/attention/ppermute | solution.py:355
  70.0 10.7 %collective-permute-done.1.one_ref = bf16[2048,128]{1,0:T(8,128)(2,1)S(1)} collective-permute-done((bf16[2048,128]{1,0:T(8,128)(2,1)S(1)}, bf16[2048,128]{1,0:T(8,128)(2,1)S(1)}, u32[]{:S(2)}, u32[]{:S(2)}) %collective-permute-start.1) | collective-permute-done | bytes 524320 | tf_op jit(solution)/shard_map/attention/ppermute | solution.py:355
  80.7 9.5 %attend_first.1 = (bf16[2048,128]{1,0:T(8,128)(2,1)}, f32[1,2048]{1,0:T(1,128)}, f32[80,2048]{1,0:T(8,128)}) custom-call(bf16[32,96,128]{2,1,0:T(8,128)(2,1)} %copy-done, bf16[384,128]{1,0:T(8,128)(2,1)} %get-tuple-element.15.text_ref, bf16[2048,128]{1,0:T(8,128)(2,1)} %bitcast.31), custom_call_target="tpu_custom_call" | custom-call | tf_op jit(solution)/shard_map/attention/attend_first/pallas_call | solution.py:137
  91.0 8.2 %attend_next.1 = (f32[1,2048]{1,0:T(1,128)}, f32[80,2048]{1,0:T(8,128)}) custom-call(bf16[2048,128]{1,0:T(8,128)(2,1)} %get-tuple-element.16.queries_ref, f32[1,2048]{1,0:T(1,128)} %get-tuple-element.17.peak_in_ref, f32[80,2048]{1,0:T(8,128)} %get-tuple-element.18.mixed_in_ref, bf16[2048,128]{1,0:T(8,128)(2,1)} %copy-done.4), custom_call_target="tpu_custom_call" | custom-call | tf_op jit(solution)/shard_map/attention/attend_next/pallas_call | solution.py:162
  100.1 14.4 %attend_last.1 = bf16[8,64,256]{2,1,0:T(8,128)(2,1)} custom-call(bf16[2048,128]{1,0:T(8,128)(2,1)} %get-tuple-element.16.queries_ref, f32[1,2048]{1,0:T(1,128)} %get-tuple-element.19.peak_in_ref, f32[80,2048]{1,0:T(8,128)} %get-tuple-element.20.mixed_in_ref, bf16[2048,128]{1,0:T(8,128)(2,1)} %copy-done.2, bf16[2048,128]{1,0:T(8,128)(2,1)} %copy-done.3), custom_call_target="tpu_custom_call" | custom-call | tf_op jit(solution)/shard_map/attention/attend_last/pallas_call | solution.py:201
  114.4 16.8 %all_to_all.11.attended_ref = bf16[8,64,256]{2,1,0:T(8,128)(2,1)} all-to-all(bf16[8,64,256]{2,1,0:T(8,128)(2,1)} %attend_last.1), channel_id=1, replica_groups=mesh['cfg'=2,'yh'=2,'z'=8,'core'=2,'uly'=4] {'z'}, dimensions={0} | all-to-all | bytes 524288 | tf_op jit(solution)/shard_map/attention/all_to_all | solution.py:406
  131.2 3.8 %project.1 = (bf16[64,2432]{1,0:T(8,128)(2,1)}, bf16[64,2432]{1,0:T(8,128)(2,1)}, bf16[64,2432]{1,0:T(8,128)(2,1)}, bf16[64,2432]{1,0:T(8,128)(2,1)}) custom-call(s32[1]{0:T(128)} %bitcast.1.place_ref, bf16[8,64,256]{2,1,0:T(8,128)(2,1)} %all_to_all.11.attended_ref, bf16[16,2,16,2432]{3,2,1,0:T(8,128)(2,1)} %bitcast.28), custom_call_target="tpu_custom_call" | custom-call | tf_op jit(solution)/shard_map/prediction/project/pallas_call | solution.py:241
  136.3 3.0 %collective-permute-start.5 = (bf16[64,2432]{1,0:T(8,128)(2,1)}, bf16[64,2432]{1,0:T(8,128)(2,1)S(1)}, u32[]{:S(2)}, u32[]{:S(2)}) collective-permute-start(bf16[64,2432]{1,0:T(8,128)(2,1)} %get-tuple-element.23), channel_id=1, source_target_pairs={{0,2},{1,3},{2,0},{3,1},{4,6},{5,7},{6,4},{7,5},{8,10},{9,11},{10,... | collective-permute-start | bytes 933896 | tf_op jit(solution)/shard_map/prediction/ppermute | solution.py:355
  142.3 3.5 %collective-permute-done.4.refs_1_ = bf16[64,2432]{1,0:T(8,128)(2,1)S(1)} collective-permute-done((bf16[64,2432]{1,0:T(8,128)(2,1)}, bf16[64,2432]{1,0:T(8,128)(2,1)S(1)}, u32[]{:S(2)}, u32[]{:S(2)}) %collective-permute-start.4) | collective-permute-done | bytes 311328 | tf_op jit(solution)/shard_map/prediction/ppermute | solution.py:355
  145.8 7.7 %collective-permute-done.5.refs_2_ = bf16[64,2432]{1,0:T(8,128)(2,1)S(1)} collective-permute-done((bf16[64,2432]{1,0:T(8,128)(2,1)}, bf16[64,2432]{1,0:T(8,128)(2,1)S(1)}, u32[]{:S(2)}, u32[]{:S(2)}) %collective-permute-start.5) | collective-permute-done | bytes 311328 | tf_op jit(solution)/shard_map/prediction/ppermute | solution.py:355
  154.4 2.8 %predict.1 = f32[64,64]{1,0:T(8,128)} custom-call(bf16[1,64,2432]{2,1,0:T(8,128)(2,1)} %stream_ref.1, f32[1,5,2432]{2,1,0:T(8,128)} %copy.28.modulation_ref, bf16[2432,64]{1,0:T(8,128)(2,1)} %copy.29.weight_ref, f32[1,64]{1,0:T(1,128)} %bitcast.36, bf16[64,2432]{1,0:T(8,128)(2,1)} %get-tuple-element.21.refs_0_, bf16[64,2432]{1,0:T(8,128)(2,1)} %copy-done.6, ...), custom_call_target="tpu_custom_call" | custom-call | tf_op jit(solution)/shard_map/prediction/predict/pallas_call | solution.py:277
  160.1 1.3 collective-permute-done.7
  161.3 1.4 fusion
  163.9 2.4 %collective-permute-start.10 = (bf16[64,64]{1,0:T(8,128)(2,1)S(1)}, bf16[64,64]{1,0:T(8,128)(2,1)S(1)}, u32[]{:S(2)}, u32[]{:S(2)}) collective-permute-start(bf16[64,64]{1,0:T(8,128)(2,1)S(1)} %get-tuple-element.25.refs_0_), channel_id=1, source_target_pairs={{0,2},{1,3},{2,0},{3,1},{4,6},{5,7},{6,4},{7,5},{8,10},{9,11},{10,... | collective-permute-start | bytes 24584 | tf_op jit(solution)/shard_map/next/ppermute | solution.py:355
  166.3 1.5 collective-permute-start.11
  168.3 6.9 %copy.31 = bf16[2,16,76,1536]{3,2,1,0:T(8,128)(2,1)} copy(bf16[2,16,76,1536]{3,2,0,1:T(8,128)(2,1)} %bitcast.27) | data formatting | bytes 14942208 | tf_op jit(solution)/shard_map/weights/transpose | solution.py:393
  175.2 8.9 %reshape.30.weight_ref = bf16[2432,1536]{1,0:T(8,128)(2,1)} reshape(bf16[2,16,76,1536]{3,2,1,0:T(8,128)(2,1)} %copy.31) | data formatting | bytes 14942208 | tf_op jit(solution)/shard_map/weights/reshape | solution.py:393
  185.4 8.1 %next_projection.1 = bf16[1,3,256,512]{3,2,1,0:T(8,128)(2,1)} custom-call(s32[1]{0:T(128)} %bitcast.1.place_ref, bf16[64,2432]{1,0:T(8,128)(2,1)} %patch_ref.1, bf16[256,2432]{1,0:T(8,128)(2,1)} %position_ref.1, f32[1,5,2432]{2,1,0:T(8,128)} %copy.28.modulation_ref, bf16[2432,1536]{1,0:T(8,128)(2,1)} %reshape.30.weight_ref, ...), custom_call_target="tpu_custom_call" | custom-call | tf_op jit(solution)/shard_map/next/next_projection/pallas_call | solution.py:328
  (64 shorter events, 14.5 us)
Async XLA Ops:
  7.2 124.1 %all-gather.5.cloned.1.call-start = ((), (), s32[]{:S(2)}) async-start(), calls=%async_computation.2 | async-start | bytes 2646016 | tf_op jit(solution)/shard_map/weights/all_gather | solution.py:389
  7.2 6.2 %collective-permute-start.3 = (bf16[16,2432]{1,0:T(8,128)(2,1)}, bf16[16,2432]{1,0:T(8,128)(2,1)S(1)}, u32[]{:S(2)}, u32[]{:S(2)}) collective-permute-start(bf16[16,2432]{1,0:T(8,128)(2,1)} %param.24), channel_id=1, source_target_pairs={{0,64},{64,0},{1,65},{65,1},{2,66},{66,2},{3,67},{67,3},{4,68},{68... | collective-permute-start | bytes 233480 | tf_op jit(solution)/shard_map/weights/ppermute | solution.py:355
  15.0 153.3 %all-gather.7.cloned.1.call-start = ((), (), s32[]{:S(2)}) async-start(), calls=%async_computation.3 | async-start | bytes 8355840 | tf_op jit(solution)/shard_map/weights/all_gather | solution.py:392
  16.4 8.1 %collective-permute-start.8 = (bf16[76,1536]{1,0:T(8,128)(2,1)S(1)}, bf16[76,1536]{1,0:T(8,128)(2,1)S(1)}, u32[]{:S(2)}, u32[]{:S(2)}) collective-permute-start(bf16[76,1536]{1,0:T(8,128)(2,1)S(1)} %bitcast.33), channel_id=1, source_target_pairs={{0,64},{64,0},{1,65},{65,1},{2,66},{66,2},{3,67},{67,3},{4,68},{68... | collective-permute-start | bytes 700424 | tf_op jit(solution)/shard_map/weights/ppermute | solution.py:355
  67.7 13.1 %copy-start = (bf16[32,96,128]{2,1,0:T(8,128)(2,1)}, bf16[32,96,128]{2,1,0:T(8,128)(2,1)S(1)}, u32[]{:S(2)}) copy-start(bf16[32,96,128]{2,1,0:T(8,128)(2,1)S(1)} %all_to_all.10.pieces_ref) | copy-start | bytes 2359300
  67.7 13.0 %copy-start.1 = (bf16[32,64,128]{2,1,0:T(8,128)(2,1)}, bf16[32,64,128]{2,1,0:T(8,128)(2,1)S(1)}, u32[]{:S(2)}) copy-start(bf16[32,64,128]{2,1,0:T(8,128)(2,1)S(1)} %slice.4) | copy-start | bytes 1572868
  67.7 13.0 %collective-permute-start.1 = (bf16[2048,128]{1,0:T(8,128)(2,1)S(1)}, bf16[2048,128]{1,0:T(8,128)(2,1)S(1)}, u32[]{:S(2)}, u32[]{:S(2)}) collective-permute-start(bf16[2048,128]{1,0:T(8,128)(2,1)S(1)} %bitcast.29), channel_id=1, source_target_pairs={{0,64},{64,0},{1,65},{65,1},{2,66},{66,2},{3,67},{67,3},{4,68},{68... | collective-permute-start | bytes 1572872 | tf_op jit(solution)/shard_map/attention/ppermute | solution.py:355
  70.0 20.2 %collective-permute-start = (bf16[2048,128]{1,0:T(8,128)(2,1)S(1)}, bf16[2048,128]{1,0:T(8,128)(2,1)S(1)}, u32[]{:S(2)}, u32[]{:S(2)}) collective-permute-start(bf16[2048,128]{1,0:T(8,128)(2,1)S(1)} %bitcast.30), channel_id=1, source_target_pairs={{0,4},{4,0},{1,5},{5,1},{2,6},{6,2},{3,7},{7,3},{8,12},{12,8},{9,1... | collective-permute-start | bytes 1572872 | tf_op jit(solution)/shard_map/attention/ppermute | solution.py:355
  80.7 18.5 %copy-start.2 = (bf16[2048,128]{1,0:T(8,128)(2,1)}, bf16[2048,128]{1,0:T(8,128)(2,1)S(1)}, u32[]{:S(2)}) copy-start(bf16[2048,128]{1,0:T(8,128)(2,1)S(1)} %collective-permute-done.1.one_ref) | copy-start | bytes 1572868
  80.7 18.5 %collective-permute-start.2 = (bf16[2048,128]{1,0:T(8,128)(2,1)S(1)}, bf16[2048,128]{1,0:T(8,128)(2,1)S(1)}, u32[]{:S(2)}, u32[]{:S(2)}) collective-permute-start(bf16[2048,128]{1,0:T(8,128)(2,1)S(1)} %collective-permute-done.1.one_ref), channel_id=1, source_target_pairs={{0,4},{4,0},{1,5},{5,1},{2,6},{6,2},{3,7},{7,3},{8,12},{12,8},{9,1... | collective-permute-start | bytes 1572872 | tf_op jit(solution)/shard_map/attention/ppermute | solution.py:355
  100.1 40.5 %copy-start.10 = (f32[1,5,2432]{2,0,1:T(1,128)S(1)}, f32[1,5,2432]{2,0,1:T(1,128)}, u32[]{:S(2)}) copy-start(f32[1,5,2432]{2,0,1:T(1,128)} %param.23) | copy-start | bytes 145924
  100.1 41.2 %copy-start.5 = (bf16[2432,64]{0,1:T(8,128)(2,1)S(1)}, bf16[2432,64]{0,1:T(8,128)(2,1)}, u32[]{:S(2)}) copy-start(bf16[2432,64]{0,1:T(8,128)(2,1)} %param.25) | copy-start | bytes 933892
  131.2 26.9 %copy-start.15 = (f32[29]{0:T(128)S(1)}, f32[29]{0:T(128)}, u32[]{:S(2)}) copy-start(f32[29]{0:T(128)} %param.28) | copy-start | bytes 352
  131.2 30.1 %copy-start.11 = (f32[64,64]{1,0:T(8,128)S(1)}, f32[64,64]{1,0:T(8,128)}, u32[]{:S(2)}) copy-start(f32[64,64]{1,0:T(8,128)} %param.27) | copy-start | bytes 49156
  131.2 36.5 %copy-start.16 = (f32[2,64]{1,0:T(2,128)S(1)}, f32[2,64]{1,0:T(2,128)}, u32[]{:S(2)}) copy-start(f32[2,64]{1,0:T(2,128)} %param.33) | copy-start | bytes 1540
  135.0 10.8 %collective-permute-start.4 = (bf16[64,2432]{1,0:T(8,128)(2,1)}, bf16[64,2432]{1,0:T(8,128)(2,1)S(1)}, u32[]{:S(2)}, u32[]{:S(2)}) collective-permute-start(bf16[64,2432]{1,0:T(8,128)(2,1)} %get-tuple-element.22), channel_id=1, source_target_pairs={{0,1},{1,2},{2,3},{3,0},{4,5},{5,6},{6,7},{7,4},{8,9},{9,10},{10,1... | collective-permute-start | bytes 933896 | tf_op jit(solution)/shard_map/prediction/ppermute | solution.py:355
  136.3 17.2 %collective-permute-start.5 = (bf16[64,2432]{1,0:T(8,128)(2,1)}, bf16[64,2432]{1,0:T(8,128)(2,1)S(1)}, u32[]{:S(2)}, u32[]{:S(2)}) collective-permute-start(bf16[64,2432]{1,0:T(8,128)(2,1)} %get-tuple-element.23), channel_id=1, source_target_pairs={{0,2},{1,3},{2,0},{3,1},{4,6},{5,7},{6,4},{7,5},{8,10},{9,11},{10,... | collective-permute-start | bytes 933896 | tf_op jit(solution)/shard_map/prediction/ppermute | solution.py:355
  139.4 14.2 %collective-permute-start.6 = (bf16[64,2432]{1,0:T(8,128)(2,1)}, bf16[64,2432]{1,0:T(8,128)(2,1)S(1)}, u32[]{:S(2)}, u32[]{:S(2)}) collective-permute-start(bf16[64,2432]{1,0:T(8,128)(2,1)} %get-tuple-element.24), channel_id=1, source_target_pairs={{0,3},{1,0},{2,1},{3,2},{4,7},{5,4},{6,5},{7,6},{8,11},{9,8},{10,9... | collective-permute-start | bytes 933896 | tf_op jit(solution)/shard_map/prediction/ppermute | solution.py:355
  145.8 7.8 %copy-start.6 = (bf16[64,2432]{1,0:T(8,128)(2,1)}, bf16[64,2432]{1,0:T(8,128)(2,1)S(1)}, u32[]{:S(2)}) copy-start(bf16[64,2432]{1,0:T(8,128)(2,1)S(1)} %collective-permute-done.4.refs_1_) | copy-start | bytes 933892
  157.2 4.1 %collective-permute-start.7 = (f32[64,64]{1,0:T(8,128)}, f32[64,64]{1,0:T(8,128)S(1)}, u32[]{:S(2)}, u32[]{:S(2)}) collective-permute-start(f32[64,64]{1,0:T(8,128)} %predict.1), channel_id=1, source_target_pairs={{0,128},{128,0},{1,129},{129,1},{2,130},{130,2},{3,131},{131,3},{4... | collective-permute-start | bytes 49160 | tf_op jit(solution)/shard_map/prediction/ppermute | solution.py:355
  162.7 12.5 %copy-start.9 = (bf16[64,64]{1,0:T(8,128)(2,1)}, bf16[64,64]{1,0:T(8,128)(2,1)S(1)}, u32[]{:S(2)}) copy-start(bf16[64,64]{1,0:T(8,128)(2,1)S(1)} %get-tuple-element.25.refs_0_) | copy-start | bytes 24580
  162.7 21.4 %collective-permute-start.9 = (bf16[64,64]{1,0:T(8,128)(2,1)S(1)}, bf16[64,64]{1,0:T(8,128)(2,1)S(1)}, u32[]{:S(2)}, u32[]{:S(2)}) collective-permute-start(bf16[64,64]{1,0:T(8,128)(2,1)S(1)} %get-tuple-element.25.refs_0_), channel_id=1, source_target_pairs={{0,1},{1,2},{2,3},{3,0},{4,5},{5,6},{6,7},{7,4},{8,9},{9,10},{10,1... | collective-permute-start | bytes 24584 | tf_op jit(solution)/shard_map/next/ppermute | solution.py:355
  163.9 20.3 %collective-permute-start.10 = (bf16[64,64]{1,0:T(8,128)(2,1)S(1)}, bf16[64,64]{1,0:T(8,128)(2,1)S(1)}, u32[]{:S(2)}, u32[]{:S(2)}) collective-permute-start(bf16[64,64]{1,0:T(8,128)(2,1)S(1)} %get-tuple-element.25.refs_0_), channel_id=1, source_target_pairs={{0,2},{1,3},{2,0},{3,1},{4,6},{5,7},{6,4},{7,5},{8,10},{9,11},{10,... | collective-permute-start | bytes 24584 | tf_op jit(solution)/shard_map/next/ppermute | solution.py:355
  166.3 17.9 %collective-permute-start.11 = (bf16[64,64]{1,0:T(8,128)(2,1)S(1)}, bf16[64,64]{1,0:T(8,128)(2,1)S(1)}, u32[]{:S(2)}, u32[]{:S(2)}) collective-permute-start(bf16[64,64]{1,0:T(8,128)(2,1)S(1)} %get-tuple-element.25.refs_0_), channel_id=1, source_target_pairs={{0,3},{1,0},{2,1},{3,2},{4,7},{5,4},{6,5},{7,6},{8,11},{9,8},{10,9... | collective-permute-start | bytes 24584 | tf_op jit(solution)/shard_map/next/ppermute | solution.py:355
  (7 other events, 5.0 us)
Sparse Core Ops, SparseCore 0:
  15.2 50.3 all-gather.4
  67.4 53.0 all-gather.6
